TPU v7x, 32 devices: a whole 2x2x4 slice. The times are simulated.
32 devices in a mesh: run: 2 (over y), tile: 4 (over z), site: 2 (over x), freq: 2 (over core).
Axes of the slice: x: 2, y: 2, z: 4, core: 2. Of those that a mesh axis runs over, the one named last changes fastest.
Arguments:
- jacobian: bfloat16 [256, 16, 8, 8, 128], P(('run', 'tile', 'site'), None, 'freq'), parts along dimension 0, may hold values from -6 to 6
- footprint: int32 [256, 16], P(('run', 'tile', 'site')), parts along dimension 0, may hold values from 0 to 4095, as said below
- home: int32 [8192], P('run'), parts along dimension 0, may hold values from 0 to 4095, as said below
- residual: float32 [256, 8, 8], P(('run', 'tile', 'site'), 'freq'), parts along dimension 0, may hold values from -6 to 6
- weights: float32 [256], P(('run', 'tile', 'site')), parts along dimension 0, may hold values from 0.2 to 2
- damping: float32 [8192, 128], P(('run', 'tile', 'site')), parts along dimension 0, may hold values from 2 to 50
- step_lengths: float32 [8], replicated, may hold values from 0.2 to 1.2
Outputs:
- model_step: float32 [8192, 128], P(('run', 'tile', 'site')), parts along dimension 0
- change: float32 [256, 8, 8], P(('run', 'tile', 'site'), 'freq'), parts along dimension 0
- curve: float32 [16, 8], P(('run', 'freq')), parts along dimension 0
There are 2 independent parts, one for each index of `run`. A program takes and returns all parts, laid end to end along the dimension named above; an argument that names none is the same for every part. Nothing has to cross between parts.
Inputs may be any that keep to these rules, and one draw needn't show every extreme that they name: home is a permutation of 0 to 4095. `footprint`: of the 256 entries of each aligned block of 16 sites, at most 64 have home[block] // 512 equal to any one value; one value receives exactly 64 entries from every such block.
All inputs are finite; a program needn't handle non-finite values.
Results may differ from a plain program's by a relative error of at most 0.0029.
Values may be sent and summed in bfloat16 or wider, within the bound.
A program may use at most 64 MiB of HBM per device.

v0:
```python
import jax
import jax.numpy as jnp
from jax import lax
from jax.sharding import PartitionSpec as P


def shards(jacobian, footprint, home, residual, weights, damping, step_lengths):
    site_count, foot_count, freq_local, comps, width = jacobian.shape
    blocks_dev = damping.shape[0]
    tiles = lax.axis_size("tile")
    groups = lax.axis_size("site")
    owner_count = tiles * groups
    entries = site_count * foot_count
    capacity = 2 * entries // owner_count
    weighted = (weights[:, None, None] * residual).astype(jnp.bfloat16)
    grad_terms = jnp.einsum(
        "skfcb,sfc->skb", jacobian, weighted, preferred_element_type=jnp.float32
    )
    curve_terms = weights[:, None, None] * jnp.sum(
        jnp.square(jacobian.astype(jnp.float32)), axis=(2, 3)
    )
    terms = jnp.concatenate([grad_terms, curve_terms], axis=-1).reshape(entries, 2 * width)
    position = home[footprint.reshape(-1)]
    dest_rank = position // blocks_dev
    local_slot = position % blocks_dev
    member = (dest_rank[:, None] == jnp.arange(owner_count, dtype=jnp.int32)[None, :]).astype(
        jnp.int32
    )
    earlier = jnp.cumsum(member, axis=0) - member
    order_in = jnp.sum(earlier * member, axis=1)
    bucket = dest_rank * capacity + order_in
    outgoing = jnp.zeros((owner_count * capacity, 2 * width), jnp.float32).at[bucket].set(terms)
    out_slots = (
        jnp.full((owner_count * capacity,), blocks_dev, jnp.int32).at[bucket].set(local_slot)
    )
    received, in_slots = (
        lax.all_to_all(
            outgoing.reshape(owner_count, capacity, 2 * width),
            ("tile", "site"),
            split_axis=0,
            concat_axis=0,
            tiled=True,
        ),
        lax.all_to_all(
            out_slots.reshape(owner_count, capacity),
            ("tile", "site"),
            split_axis=0,
            concat_axis=0,
            tiled=True,
        ),
    )
    flat_slots = in_slots.reshape(-1)
    totals = jax.ops.segment_sum(
        received.reshape(-1, 2 * width), flat_slots, num_segments=blocks_dev + 1
    )[:blocks_dev]
    totals = lax.psum(totals, "freq")
    model_step = totals[:, :width] / (totals[:, width:] + damping)
    step_low = jnp.concatenate(
        [model_step.astype(jnp.bfloat16), jnp.zeros((1, width), jnp.bfloat16)], axis=0
    )
    reply = step_low[flat_slots]
    returned = lax.all_to_all(
        reply.reshape(owner_count, capacity, width),
        ("tile", "site"),
        split_axis=0,
        concat_axis=0,
        tiled=True,
    )
    entry_rows = returned.reshape(owner_count * capacity, width)[bucket]
    entry_step = entry_rows.reshape(site_count, foot_count, width)
    change = jnp.einsum("skfcb,skb->sfc", jacobian, entry_step, preferred_element_type=jnp.float32)
    scale_total = site_count * owner_count * comps
    gap = residual[:, :, :, None] - step_lengths[None, None, None, :] * change[:, :, :, None]
    partial_sum = jnp.einsum("s,sfca->fa", weights, gap * gap)
    curve = lax.psum(partial_sum, ("tile", "site")) / scale_total
    return (model_step, change, curve)


def solution(mesh):
    placed = (
        P(("run", "tile", "site"), None, "freq", None, None),
        P(("run", "tile", "site"), None),
        P("run"),
        P(("run", "tile", "site"), "freq", None),
        P(("run", "tile", "site")),
        P(("run", "tile", "site"), None),
        P(),
    )
    return jax.shard_map(
        shards,
        mesh=mesh,
        in_specs=placed,
        out_specs=(
            P(("run", "tile", "site"), None),
            P(("run", "tile", "site"), "freq", None),
            P(("run", "freq"), None),
        ),
        check_vma=False,
    )
```

profile of v0, /device:TPU:0, one launch (start us, length us, event | category | flops | bytes accessed | tf_op | source)
XLA Modules:
  0.0 117.0 jit_solution(13052791357690887810)
XLA Ops:
  7.2 0.9 reshape.181
  8.2 1.7 %gather_fusion = s32[256]{0:T(256)S(1)} fusion(s32[4096]{0:T(1024)S(1)} %copy-done, s32[1024]{0:T(1024)S(1)} %pad_clamp_fusion.2), kind=kCustom, calls=%fused_computation | custom fusion | bytes 3072 | tf_op jit(solution)/shard_map/gather | solution.py:23
  9.9 0.6 reduce-window.6
  10.9 1.4 %scatter_custom_fusion = s32[512]{0:T(512)S(1)} fusion(s32[256]{0:T(256)S(1)} %bitcast.64, s32[256]{0:T(256)S(1)} %get-tuple-element.5, s32[]{:T(128)} %constant.41.clone.1), kind=kCustom, calls=%fused_computation.49 | custom fusion | bytes 2052 | tf_op jit(solution)/shard_map/scatter | solution.py:34
  12.3 0.7 all_to_all.12
  13.0 7.3 %all-to-all-start = ((s32[8,1,64]{2,1,0:T(1,128)}), s32[8,1,64]{2,1,0:T(1,128)S(1)}, u32[]{:S(2)}, u32[]{:S(2)}) async-start(s32[8,1,64]{2,1,0:T(1,128)} %all_to_all.12), calls=%async_computation | async-start | bytes 8192 | tf_op jit(solution)/shard_map/all_to_all | solution.py:44
  20.2 2.3 %multiply_reduce_fusion = f32[16,16,128]{2,1,0:T(8,128)S(1)} fusion(bf16[16,16,4,8,128]{4,3,2,1,0:T(8,128)(2,1)} %param.7), kind=kLoop, calls=%fused_computation.6 | loop fusion | flops 3112960 | bytes 2228224 | tf_op jit(solution)/shard_map/reduce_sum | solution.py:19
  22.8 0.6 fusion.22
  23.4 2.2 %scatter_custom_fusion.1 = f32[512,256]{1,0:T(8,128)} fusion(s32[256]{0:T(256)S(1)} %bitcast.65, f32[256,256]{1,0:T(8,128)S(1)} %bitcast.56, f32[]{:T(128)} %constant.40.clone.1), kind=kCustom, calls=%fused_computation.14 | custom fusion | bytes 524292 | tf_op jit(solution)/shard_map/scatter | solution.py:32
  25.6 1.0 all-to-all-done
  26.6 5.0 %all-to-all-start.1 = ((f32[8,64,256]{2,1,0:T(8,128)}), f32[8,64,256]{2,1,0:T(8,128)S(1)}, u32[]{:S(2)}, u32[]{:S(2)}) async-start(f32[8,64,256]{2,1,0:T(8,128)} %bitcast.11), calls=%async_computation.1 | async-start | bytes 1048576 | tf_op jit(solution)/shard_map/all_to_all | solution.py:37
  32.2 0.7 reduce.7
  32.9 12.7 %all-to-all-done.1 = f32[8,64,256]{2,1,0:T(8,128)S(1)} async-done(((f32[8,64,256]{2,1,0:T(8,128)}), f32[8,64,256]{2,1,0:T(8,128)S(1)}, u32[]{:S(2)}, u32[]{:S(2)}) %all-to-all-start.1) | async-done | bytes 524320 | tf_op jit(solution)/shard_map/all_to_all | solution.py:37
  45.6 3.7 %scatter_custom_fusion.2 = f32[513,256]{1,0:T(8,128)S(1)} fusion(s32[512]{0:T(512)S(1)} %reshape.231, f32[512,256]{1,0:T(8,128)S(1)} %bitcast.54, f32[]{:T(128)} %constant.40.clone.1), kind=kCustom, calls=%fused_computation.9 | custom fusion | flops 131072 | bytes 525316 | tf_op jit(solution)/shard_map/scatter-add | solution.py:53
  49.3 0.8 slice.27
  50.2 17.9 %all-reduce.3.cloned.1.call-done = f32[512,256]{1,0:T(8,128)} async-done(((f32[512,256]{1,0:T(8,128)}), f32[512,256]{1,0:T(8,128)}) %all-reduce.3.cloned.1.call-update) | async-done | bytes 524304 | tf_op jit(solution)/shard_map/psum | solution.py:56
  68.1 1.8 %fusion.17 = (bf16[512,128]{1,0:T(8,128)(2,1)S(1)}, f32[512,128]{1,0:T(8,128)}) fusion(f32[512,128]{1,0:T(8,128)S(1)} %copy-done.2, f32[512,256]{1,0:T(8,128)} %all-reduce.3.cloned.1.call-done), kind=kLoop, calls=%fused_computation.55 | loop fusion | flops 196608 | bytes 1179648 | tf_op jit(solution)/shard_map/convert_element_type | solution.py:59
  69.9 1.9 %gather_fusion.1 = bf16[512,128]{1,0:T(8,128)(2,1)} fusion(bf16[513,128]{1,0:T(8,128)(2,1)S(1)} %concatenate.7, s32[1024]{0:T(1024)S(1)} %pad_clamp_fusion.1), kind=kCustom, calls=%fused_computation.1 | custom fusion | bytes 264192 | tf_op jit(solution)/shard_map/gather | solution.py:61
  71.8 5.8 %all-to-all-start.2 = ((bf16[8,64,128]{2,1,0:T(8,128)(2,1)}), bf16[8,64,128]{2,1,0:T(8,128)(2,1)S(1)}, u32[]{:S(2)}, u32[]{:S(2)}) async-start(bf16[8,64,128]{2,1,0:T(8,128)(2,1)} %bitcast.14), calls=%async_computation.2 | async-start | bytes 262144 | tf_op jit(solution)/shard_map/all_to_all | solution.py:62
  77.6 7.4 %all-to-all-done.2 = bf16[8,64,128]{2,1,0:T(8,128)(2,1)S(1)} async-done(((bf16[8,64,128]{2,1,0:T(8,128)(2,1)}), bf16[8,64,128]{2,1,0:T(8,128)(2,1)S(1)}, u32[]{:S(2)}, u32[]{:S(2)}) %all-to-all-start.2) | async-done | bytes 131104 | tf_op jit(solution)/shard_map/all_to_all | solution.py:62
  85.1 0.9 gather_fusion.2
  85.9 4.7 %fusion = f32[16,1,4,8,1]{3,1,4,2,0:T(1,128)S(1)} fusion(bf16[16,16,4,8,128]{4,3,2,1,0:T(8,128)(2,1)S(1)} %copy-done.1, bf16[16,16,128,1,1]{2,1,0,3,4:T(8,128)(2,1)S(1)} %bitcast.57), kind=kOutput, calls=%fused_computation.7 | convolution fusion | flops 2097152 | bytes 2164736 | tf_op jit(solution)/shard_map/skfcb,skb->sfc/dot_general | solution.py:71
  91.0 18.6 %psum.15 = f32[4,8]{1,0:T(4,128)S(1)} all-reduce(f32[4,8]{1,0:T(4,128)S(1)} %bitcast.63), channel_id=1, replica_groups=mesh['run'=2,'tile'=4,'site'=2,'freq'=2] {'tile','site'}, use_global_device_ids=true, to_apply=%region_9.10 | all-reduce | flops 32 | bytes 256 | tf_op jit(solution)/shard_map/psum | solution.py:75
  109.5 0.6 broadcast_multiply_fusion.1
  (40 shorter events, 1.7 us)
Async XLA Ops:
  7.2 1.0 copy-start
  7.2 15.6 %copy-start.1 = (bf16[16,16,4,8,128]{4,3,2,1,0:T(8,128)(2,1)S(1)}, bf16[16,16,4,8,128]{4,3,2,1,0:T(8,128)(2,1)}, u32[]{:S(2)}) copy-start(bf16[16,16,4,8,128]{4,3,2,1,0:T(8,128)(2,1)} %param.7) | copy-start | bytes 6291460
  7.2 15.4 %copy-start.5 = (f32[16]{0:T(128)S(1)}, f32[16]{0:T(128)}, u32[]{:S(2)}) copy-start(f32[16]{0:T(128)} %param.11) | copy-start | bytes 196
  7.2 15.5 %copy-start.4 = (f32[16,4,8]{0,2,1:T(8,128)S(1)}, f32[16,4,8]{0,2,1:T(8,128)}, u32[]{:S(2)}) copy-start(f32[16,4,8]{0,2,1:T(8,128)} %param.10) | copy-start | bytes 6148
  13.0 13.6 %all-to-all-start = ((s32[8,1,64]{2,1,0:T(1,128)}), s32[8,1,64]{2,1,0:T(1,128)S(1)}, u32[]{:S(2)}, u32[]{:S(2)}) async-start(s32[8,1,64]{2,1,0:T(1,128)} %all_to_all.12), calls=%async_computation | async-start | bytes 8192 | tf_op jit(solution)/shard_map/all_to_all | solution.py:44
  23.4 44.7 %copy-start.2 = (f32[512,128]{1,0:T(8,128)S(1)}, f32[512,128]{1,0:T(8,128)}, u32[]{:S(2)}) copy-start(f32[512,128]{1,0:T(8,128)} %param.12) | copy-start | bytes 786436
  26.6 19.0 %all-to-all-start.1 = ((f32[8,64,256]{2,1,0:T(8,128)}), f32[8,64,256]{2,1,0:T(8,128)S(1)}, u32[]{:S(2)}, u32[]{:S(2)}) async-start(f32[8,64,256]{2,1,0:T(8,128)} %bitcast.11), calls=%async_computation.1 | async-start | bytes 1048576 | tf_op jit(solution)/shard_map/all_to_all | solution.py:37
  31.6 36.5 %all-reduce.3.cloned.1.call-start = ((), (), s32[]{:S(2)}) async-start(), calls=%async_computation.3 | async-start | bytes 1048576 | tf_op jit(solution)/shard_map/psum | solution.py:56
  71.8 13.2 %all-to-all-start.2 = ((bf16[8,64,128]{2,1,0:T(8,128)(2,1)}), bf16[8,64,128]{2,1,0:T(8,128)(2,1)S(1)}, u32[]{:S(2)}, u32[]{:S(2)}) async-start(bf16[8,64,128]{2,1,0:T(8,128)(2,1)} %bitcast.14), calls=%async_computation.2 | async-start | bytes 262144 | tf_op jit(solution)/shard_map/all_to_all | solution.py:62
  85.1 5.6 %copy-start.6 = (f32[8]{0:T(128)S(1)}, f32[8]{0:T(128)}, u32[]{:S(2)}) copy-start(f32[8]{0:T(128)} %param.13) | copy-start | bytes 100
  90.7 19.4 %copy-start.3 = (f32[16,1,4,8,1]{0,3,2,1,4:T(8,128)}, f32[16,1,4,8,1]{0,3,2,1,4:T(8,128)S(1)}, u32[]{:S(2)}) copy-start(f32[16,1,4,8,1]{0,3,2,1,4:T(8,128)S(1)} %copy.18) | copy-start | bytes 6148
Sparse Core Ops, SparseCore 0:
  50.3 17.8 all-reduce.2
where the time goes:
time: 117 us
  waiting for transfers between devices  39 us (33%)
  blocking collectives  18.6 us (16%)
  starting transfers between devices  18.1 us (15%)
  between operations  14.2 us (12%)
  local copies, waits for them, and re-layouts  11.6 us (10%)
  other arithmetic  10.1 us (9%)
  matrix products  5.41 us (5%)
    psum x1, blocking collectives, shards(): curve = lax.psum(partial_sum, ('tile', 'site')) / scale_total  18.6 us
    psum x1, waiting for transfers between devices, shards(): totals = lax.psum(totals, 'freq')  17.9 us
    all_to_all x1, waiting for transfers between devices, shards(): lax.all_to_all(outgoing.reshape(owner_count, capacity, 2 * width), ('tile...  12.7 us
    all_to_all x1, waiting for transfers between devices, shards(): lax.all_to_all(reply.reshape(owner_count, capacity, width), ('tile', 'sit...  7.43 us
    all_to_all x1, starting transfers between devices, shards(): lax.all_to_all(out_slots.reshape(owner_count, capacity), ('tile', 'site')...  7.25 us
    all_to_all x1, starting transfers between devices, shards(): lax.all_to_all(reply.reshape(owner_count, capacity, width), ('tile', 'sit...  5.78 us
    all_to_all x1, starting transfers between devices, shards(): lax.all_to_all(outgoing.reshape(owner_count, capacity, 2 * width), ('tile...  5 us
    dot_general x1, matrix products, shards(): jnp.einsum('skfcb,skb->sfc', jacobian, entry_step, preferred_element_type...  4.69 us
  transfers between devices with their start and end apart: 4, of which 4 were waited for; matrix products, arithmetic and copies ran while one was open for 6% of the time, Pallas kernels for 0%

commit v1 on v0

--- a/solution.py
+++ b/solution.py
@@ -2,6 +2,22 @@
 import jax.numpy as jnp
 from jax import lax
 from jax.sharding import PartitionSpec as P
+
+
+def pairwise_exchange(array, axis, split, join):
+    ways, here = (lax.axis_size(axis), lax.axis_index(axis))
+    width = array.shape[split] // ways
+    dims = list(array.shape)
+    dims[split] = width
+    height = dims[join]
+    dims[join] = height * ways
+    full = jnp.zeros(dims, array.dtype)
+    for mask in range(ways):
+        part = lax.dynamic_slice_in_dim(array, (here ^ mask) * width, width, axis=split)
+        if mask:
+            part = lax.ppermute(part, axis, [(d, d ^ mask) for d in range(ways)])
+        full = lax.dynamic_update_slice_in_dim(full, part, (here ^ mask) * height, axis=join)
+    return full
 
 
 def shards(jacobian, footprint, home, residual, weights, damping, step_lengths):
@@ -59,12 +75,8 @@
         [model_step.astype(jnp.bfloat16), jnp.zeros((1, width), jnp.bfloat16)], axis=0
     )
     reply = step_low[flat_slots]
-    returned = lax.all_to_all(
-        reply.reshape(owner_count, capacity, width),
-        ("tile", "site"),
-        split_axis=0,
-        concat_axis=0,
-        tiled=True,
+    returned = pairwise_exchange(
+        reply.reshape(owner_count, capacity, width), ("tile", "site"), 0, 0
     )
     entry_rows = returned.reshape(owner_count * capacity, width)[bucket]
     entry_step = entry_rows.reshape(site_count, foot_count, width)

time: 117 us -> 120 us (1.026)
  starting transfers between devices: 18.1 us -> 23.5 us
  waiting for transfers between devices: 39 us -> 37.7 us
    ppermute x0 -> x7, starting transfers between devices: none -> 11.2 us  [pairwise_exchange(): part = lax.ppermute(part, axis, [(d, d ^ mask) for d in range(ways)])]
    all_to_all x1 -> x0, waiting for transfers between devices: 7.43 us -> none  [shards(): lax.all_to_all(reply.reshape(owner_count, capacity, width), ('tile', 'sit...]
    ppermute x0 -> x7, waiting for transfers between devices: none -> 6.17 us  [pairwise_exchange(): part = lax.ppermute(part, axis, [(d, d ^ mask) for d in range(ways)])]
    all_to_all x1 -> x0, starting transfers between devices: 5.78 us -> none  [shards(): lax.all_to_all(reply.reshape(owner_count, capacity, width), ('tile', 'sit...]
  transfers between devices with their start and end apart: 4 -> 10, of which waited for: 4 -> 6; matrix products, arithmetic and copies ran while one was open for 6% -> 6% of each run, Pallas kernels for 0% -> 0%
where the time goes in v1:
time: 120 us
  waiting for transfers between devices  37.7 us (31%)
  starting transfers between devices  23.5 us (20%)
  blocking collectives  17.7 us (15%)
  between operations  14.3 us (12%)
  local copies, waits for them, and re-layouts  11.2 us (9%)
  other arithmetic  10.1 us (8%)
  matrix products  5.41 us (5%)
    psum x1, waiting for transfers between devices, shards(): totals = lax.psum(totals, 'freq')  17.9 us
    psum x1, blocking collectives, shards(): curve = lax.psum(partial_sum, ('tile', 'site')) / scale_total  17.7 us
    all_to_all x1, waiting for transfers between devices, shards(): lax.all_to_all(outgoing.reshape(owner_count, capacity, 2 * width), ('tile...  12.7 us
    ppermute x7, starting transfers between devices, pairwise_exchange(): part = lax.ppermute(part, axis, [(d, d ^ mask) for d in range(ways)])  11.2 us
    all_to_all x1, starting transfers between devices, shards(): lax.all_to_all(out_slots.reshape(owner_count, capacity), ('tile', 'site')...  7.25 us
    ppermute x7, waiting for transfers between devices, pairwise_exchange(): part = lax.ppermute(part, axis, [(d, d ^ mask) for d in range(ways)])  6.17 us
    all_to_all x1, starting transfers between devices, shards(): lax.all_to_all(outgoing.reshape(owner_count, capacity, 2 * width), ('tile...  5 us
    dot_general x1, matrix products, shards(): jnp.einsum('skfcb,skb->sfc', jacobian, entry_step, preferred_element_type...  4.69 us
  transfers between devices with their start and end apart: 10, of which 6 were waited for; matrix products, arithmetic and copies ran while one was open for 6% of the time, Pallas kernels for 0%

profile of v1, /device:TPU:0, one launch (start us, length us, event | category | flops | bytes accessed | tf_op | source)
XLA Modules:
  0.0 119.8 jit_solution(16791874342603576307)
XLA Ops:
  7.2 0.9 reshape.181
  8.2 1.7 %gather_fusion = s32[256]{0:T(256)S(1)} fusion(s32[4096]{0:T(1024)S(1)} %copy-done, s32[1024]{0:T(1024)S(1)} %pad_clamp_fusion.2), kind=kCustom, calls=%fused_computation | custom fusion | bytes 3072 | tf_op jit(solution)/shard_map/gather | solution.py:39
  10.9 1.4 %scatter_custom_fusion = s32[512]{0:T(512)S(1)} fusion(s32[256]{0:T(256)S(1)} %bitcast.65, s32[256]{0:T(256)S(1)} %get-tuple-element.13, s32[]{:T(128)} %constant.25.clone.1), kind=kCustom, calls=%fused_computation.64 | custom fusion | bytes 2052 | tf_op jit(solution)/shard_map/scatter | solution.py:50
  13.0 7.3 %all-to-all-start = ((s32[8,1,64]{2,1,0:T(1,128)}), s32[8,1,64]{2,1,0:T(1,128)S(1)}, u32[]{:S(2)}, u32[]{:S(2)}) async-start(s32[8,1,64]{2,1,0:T(1,128)} %all_to_all.9), calls=%async_computation | async-start | bytes 8192 | tf_op jit(solution)/shard_map/all_to_all | solution.py:60
  20.2 2.3 %multiply_reduce_fusion = f32[16,16,128]{2,1,0:T(8,128)S(1)} fusion(bf16[16,16,4,8,128]{4,3,2,1,0:T(8,128)(2,1)} %param.7), kind=kLoop, calls=%fused_computation.6 | loop fusion | flops 3112960 | bytes 2228224 | tf_op jit(solution)/shard_map/reduce_sum | solution.py:35
  23.4 2.2 %scatter_custom_fusion.1 = f32[512,256]{1,0:T(8,128)} fusion(s32[256]{0:T(256)S(1)} %bitcast.66, f32[256,256]{1,0:T(8,128)S(1)} %bitcast.57, f32[]{:T(128)} %constant.24.clone.1), kind=kCustom, calls=%fused_computation.14 | custom fusion | bytes 524292 | tf_op jit(solution)/shard_map/scatter | solution.py:48
  25.6 1.0 all-to-all-done
  26.6 5.0 %all-to-all-start.1 = ((f32[8,64,256]{2,1,0:T(8,128)}), f32[8,64,256]{2,1,0:T(8,128)S(1)}, u32[]{:S(2)}, u32[]{:S(2)}) async-start(f32[8,64,256]{2,1,0:T(8,128)} %bitcast.11), calls=%async_computation.1 | async-start | bytes 1048576 | tf_op jit(solution)/shard_map/all_to_all | solution.py:53
  32.9 12.7 %all-to-all-done.1 = f32[8,64,256]{2,1,0:T(8,128)S(1)} async-done(((f32[8,64,256]{2,1,0:T(8,128)}), f32[8,64,256]{2,1,0:T(8,128)S(1)}, u32[]{:S(2)}, u32[]{:S(2)}) %all-to-all-start.1) | async-done | bytes 524320 | tf_op jit(solution)/shard_map/all_to_all | solution.py:53
  45.6 3.7 %scatter_custom_fusion.2 = f32[513,256]{1,0:T(8,128)S(1)} fusion(s32[512]{0:T(512)S(1)} %reshape.231, f32[512,256]{1,0:T(8,128)S(1)} %bitcast.55, f32[]{:T(128)} %constant.24.clone.1), kind=kCustom, calls=%fused_computation.9 | custom fusion | flops 131072 | bytes 525316 | tf_op jit(solution)/shard_map/scatter-add | solution.py:69
  49.3 0.8 slice.27
  50.3 17.9 %all-reduce.3.cloned.1.call-done = f32[512,256]{1,0:T(8,128)} async-done(((f32[512,256]{1,0:T(8,128)}), f32[512,256]{1,0:T(8,128)}) %all-reduce.3.cloned.1.call-update) | async-done | bytes 524304 | tf_op jit(solution)/shard_map/psum | solution.py:72
  68.1 1.8 %fusion.17 = (bf16[512,128]{1,0:T(8,128)(2,1)S(1)}, f32[512,128]{1,0:T(8,128)}) fusion(f32[512,128]{1,0:T(8,128)S(1)} %copy-done.2, f32[512,256]{1,0:T(8,128)} %all-reduce.3.cloned.1.call-done), kind=kLoop, calls=%fused_computation.70 | loop fusion | flops 196608 | bytes 1179648 | tf_op jit(solution)/shard_map/convert_element_type | solution.py:75
  69.9 1.3 %gather_fusion.1 = bf16[512,128]{1,0:T(8,128)(2,1)S(1)} fusion(bf16[513,128]{1,0:T(8,128)(2,1)S(1)} %concatenate.7, s32[1024]{0:T(1024)S(1)} %pad_clamp_fusion.1), kind=kCustom, calls=%fused_computation.1 | custom fusion | bytes 264192 | tf_op jit(solution)/shard_map/gather | solution.py:77
  71.4 1.8 %collective-permute-start = (bf16[1,64,128]{2,1,0:T(8,128)(2,1)S(1)}, bf16[1,64,128]{2,1,0:T(8,128)(2,1)S(1)}, u32[]{:S(2)}, u32[]{:S(2)}) collective-permute-start(bf16[1,64,128]{2,1,0:T(8,128)(2,1)S(1)} %get-tuple-element.11), channel_id=1, source_target_pairs={{0,2},{2,0},{4,6},{6,4},{8,10},{10,8},{12,14},{14,12},{1,3},{3,1},... | collective-permute-start | bytes 49160 | tf_op jit(solution)/shard_map/ppermute | solution.py:18
  73.2 1.5 %collective-permute-start.1 = (bf16[1,64,128]{2,1,0:T(8,128)(2,1)S(1)}, bf16[1,64,128]{2,1,0:T(8,128)(2,1)S(1)}, u32[]{:S(2)}, u32[]{:S(2)}) collective-permute-start(bf16[1,64,128]{2,1,0:T(8,128)(2,1)S(1)} %get-tuple-element.10), channel_id=1, source_target_pairs={{0,4},{2,6},{4,0},{6,2},{8,12},{10,14},{12,8},{14,10},{1,5},{3,7},... | collective-permute-start | bytes 49160 | tf_op jit(solution)/shard_map/ppermute | solution.py:18
  74.9 2.7 %collective-permute-start.3 = (bf16[1,64,128]{2,1,0:T(8,128)(2,1)S(1)}, bf16[1,64,128]{2,1,0:T(8,128)(2,1)S(1)}, u32[]{:S(2)}, u32[]{:S(2)}) collective-permute-start(bf16[1,64,128]{2,1,0:T(8,128)(2,1)S(1)} %get-tuple-element.8), channel_id=1, source_target_pairs={{0,8},{2,10},{4,12},{6,14},{8,0},{10,2},{12,4},{14,6},{1,9},{3,11}... | collective-permute-start | bytes 49160 | tf_op jit(solution)/shard_map/ppermute | solution.py:18
  77.6 1.4 %collective-permute-start.4 = (bf16[1,64,128]{2,1,0:T(8,128)(2,1)S(1)}, bf16[1,64,128]{2,1,0:T(8,128)(2,1)S(1)}, u32[]{:S(2)}, u32[]{:S(2)}) collective-permute-start(bf16[1,64,128]{2,1,0:T(8,128)(2,1)S(1)} %get-tuple-element.7), channel_id=1, source_target_pairs={{0,10},{2,8},{4,14},{6,12},{8,2},{10,0},{12,6},{14,4},{1,11},{3,9}... | collective-permute-start | bytes 49160 | tf_op jit(solution)/shard_map/ppermute | solution.py:18
  79.0 3.3 %collective-permute-start.5 = (bf16[1,64,128]{2,1,0:T(8,128)(2,1)S(1)}, bf16[1,64,128]{2,1,0:T(8,128)(2,1)S(1)}, u32[]{:S(2)}, u32[]{:S(2)}) collective-permute-start(bf16[1,64,128]{2,1,0:T(8,128)(2,1)S(1)} %get-tuple-element.6), channel_id=1, source_target_pairs={{0,12},{2,14},{4,8},{6,10},{8,4},{10,6},{12,0},{14,2},{1,13},{3,15... | collective-permute-start | bytes 49160 | tf_op jit(solution)/shard_map/ppermute | solution.py:18
  83.1 1.4 %collective-permute-done.5 = bf16[1,64,128]{2,1,0:T(8,128)(2,1)S(1)} collective-permute-done((bf16[1,64,128]{2,1,0:T(8,128)(2,1)S(1)}, bf16[1,64,128]{2,1,0:T(8,128)(2,1)S(1)}, u32[]{:S(2)}, u32[]{:S(2)}) %collective-permute-start.5) | collective-permute-done | bytes 16416 | tf_op jit(solution)/shard_map/ppermute | solution.py:18
  84.6 4.2 %collective-permute-done.6 = bf16[1,64,128]{2,1,0:T(8,128)(2,1)S(1)} collective-permute-done((bf16[1,64,128]{2,1,0:T(8,128)(2,1)S(1)}, bf16[1,64,128]{2,1,0:T(8,128)(2,1)S(1)}, u32[]{:S(2)}, u32[]{:S(2)}) %collective-permute-start.6) | collective-permute-done | bytes 16416 | tf_op jit(solution)/shard_map/ppermute | solution.py:18
  88.8 0.9 gather_fusion.2
  89.7 4.7 %fusion = f32[16,1,4,8,1]{3,1,4,2,0:T(1,128)S(1)} fusion(bf16[16,16,4,8,128]{4,3,2,1,0:T(8,128)(2,1)S(1)} %copy-done.1, bf16[16,16,128,1,1]{2,1,0,3,4:T(8,128)(2,1)S(1)} %bitcast.58), kind=kOutput, calls=%fused_computation.7 | convolution fusion | flops 2097152 | bytes 2164736 | tf_op jit(solution)/shard_map/skfcb,skb->sfc/dot_general | solution.py:83
  94.7 17.7 %psum.15 = f32[4,8]{1,0:T(4,128)S(1)} all-reduce(f32[4,8]{1,0:T(4,128)S(1)} %bitcast.64), channel_id=1, replica_groups=mesh['run'=2,'tile'=4,'site'=2,'freq'=2] {'tile','site'}, use_global_device_ids=true, to_apply=%region_9.10 | all-reduce | flops 32 | bytes 256 | tf_op jit(solution)/shard_map/psum | solution.py:87
  (61 shorter events, 5.9 us)
Async XLA Ops:
  7.2 1.0 copy-start
  7.2 15.6 %copy-start.1 = (bf16[16,16,4,8,128]{4,3,2,1,0:T(8,128)(2,1)S(1)}, bf16[16,16,4,8,128]{4,3,2,1,0:T(8,128)(2,1)}, u32[]{:S(2)}) copy-start(bf16[16,16,4,8,128]{4,3,2,1,0:T(8,128)(2,1)} %param.7) | copy-start | bytes 6291460
  7.2 15.4 %copy-start.5 = (f32[16]{0:T(128)S(1)}, f32[16]{0:T(128)}, u32[]{:S(2)}) copy-start(f32[16]{0:T(128)} %param.11) | copy-start | bytes 196
  7.2 15.5 %copy-start.4 = (f32[16,4,8]{0,2,1:T(8,128)S(1)}, f32[16,4,8]{0,2,1:T(8,128)}, u32[]{:S(2)}) copy-start(f32[16,4,8]{0,2,1:T(8,128)} %param.10) | copy-start | bytes 6148
  13.0 13.6 %all-to-all-start = ((s32[8,1,64]{2,1,0:T(1,128)}), s32[8,1,64]{2,1,0:T(1,128)S(1)}, u32[]{:S(2)}, u32[]{:S(2)}) async-start(s32[8,1,64]{2,1,0:T(1,128)} %all_to_all.9), calls=%async_computation | async-start | bytes 8192 | tf_op jit(solution)/shard_map/all_to_all | solution.py:60
  23.4 44.7 %copy-start.2 = (f32[512,128]{1,0:T(8,128)S(1)}, f32[512,128]{1,0:T(8,128)}, u32[]{:S(2)}) copy-start(f32[512,128]{1,0:T(8,128)} %param.12) | copy-start | bytes 786436
  26.6 19.0 %all-to-all-start.1 = ((f32[8,64,256]{2,1,0:T(8,128)}), f32[8,64,256]{2,1,0:T(8,128)S(1)}, u32[]{:S(2)}, u32[]{:S(2)}) async-start(f32[8,64,256]{2,1,0:T(8,128)} %bitcast.11), calls=%async_computation.1 | async-start | bytes 1048576 | tf_op jit(solution)/shard_map/all_to_all | solution.py:53
  31.6 36.5 %all-reduce.3.cloned.1.call-start = ((), (), s32[]{:S(2)}) async-start(), calls=%async_computation.2 | async-start | bytes 1048576 | tf_op jit(solution)/shard_map/psum | solution.py:72
  71.4 7.7 %collective-permute-start = (bf16[1,64,128]{2,1,0:T(8,128)(2,1)S(1)}, bf16[1,64,128]{2,1,0:T(8,128)(2,1)S(1)}, u32[]{:S(2)}, u32[]{:S(2)}) collective-permute-start(bf16[1,64,128]{2,1,0:T(8,128)(2,1)S(1)} %get-tuple-element.11), channel_id=1, source_target_pairs={{0,2},{2,0},{4,6},{6,4},{8,10},{10,8},{12,14},{14,12},{1,3},{3,1},... | collective-permute-start | bytes 49160 | tf_op jit(solution)/shard_map/ppermute | solution.py:18
  73.2 9.2 %collective-permute-start.1 = (bf16[1,64,128]{2,1,0:T(8,128)(2,1)S(1)}, bf16[1,64,128]{2,1,0:T(8,128)(2,1)S(1)}, u32[]{:S(2)}, u32[]{:S(2)}) collective-permute-start(bf16[1,64,128]{2,1,0:T(8,128)(2,1)S(1)} %get-tuple-element.10), channel_id=1, source_target_pairs={{0,4},{2,6},{4,0},{6,2},{8,12},{10,14},{12,8},{14,10},{1,5},{3,7},... | collective-permute-start | bytes 49160 | tf_op jit(solution)/shard_map/ppermute | solution.py:18
  74.7 7.9 %collective-permute-start.2 = (bf16[1,64,128]{2,1,0:T(8,128)(2,1)S(1)}, bf16[1,64,128]{2,1,0:T(8,128)(2,1)S(1)}, u32[]{:S(2)}, u32[]{:S(2)}) collective-permute-start(bf16[1,64,128]{2,1,0:T(8,128)(2,1)S(1)} %get-tuple-element.9), channel_id=1, source_target_pairs={{0,6},{2,4},{4,2},{6,0},{8,14},{10,12},{12,10},{14,8},{1,7},{3,5},... | collective-permute-start | bytes 49160 | tf_op jit(solution)/shard_map/ppermute | solution.py:18
  74.9 7.7 %collective-permute-start.3 = (bf16[1,64,128]{2,1,0:T(8,128)(2,1)S(1)}, bf16[1,64,128]{2,1,0:T(8,128)(2,1)S(1)}, u32[]{:S(2)}, u32[]{:S(2)}) collective-permute-start(bf16[1,64,128]{2,1,0:T(8,128)(2,1)S(1)} %get-tuple-element.8), channel_id=1, source_target_pairs={{0,8},{2,10},{4,12},{6,14},{8,0},{10,2},{12,4},{14,6},{1,9},{3,11}... | collective-permute-start | bytes 49160 | tf_op jit(solution)/shard_map/ppermute | solution.py:18
  77.6 5.5 %collective-permute-start.4 = (bf16[1,64,128]{2,1,0:T(8,128)(2,1)S(1)}, bf16[1,64,128]{2,1,0:T(8,128)(2,1)S(1)}, u32[]{:S(2)}, u32[]{:S(2)}) collective-permute-start(bf16[1,64,128]{2,1,0:T(8,128)(2,1)S(1)} %get-tuple-element.7), channel_id=1, source_target_pairs={{0,10},{2,8},{4,14},{6,12},{8,2},{10,0},{12,6},{14,4},{1,11},{3,9}... | collective-permute-start | bytes 49160 | tf_op jit(solution)/shard_map/ppermute | solution.py:18
  79.0 5.5 %collective-permute-start.5 = (bf16[1,64,128]{2,1,0:T(8,128)(2,1)S(1)}, bf16[1,64,128]{2,1,0:T(8,128)(2,1)S(1)}, u32[]{:S(2)}, u32[]{:S(2)}) collective-permute-start(bf16[1,64,128]{2,1,0:T(8,128)(2,1)S(1)} %get-tuple-element.6), channel_id=1, source_target_pairs={{0,12},{2,14},{4,8},{6,10},{8,4},{10,6},{12,0},{14,2},{1,13},{3,15... | collective-permute-start | bytes 49160 | tf_op jit(solution)/shard_map/ppermute | solution.py:18
  82.4 6.4 %collective-permute-start.6 = (bf16[1,64,128]{2,1,0:T(8,128)(2,1)S(1)}, bf16[1,64,128]{2,1,0:T(8,128)(2,1)S(1)}, u32[]{:S(2)}, u32[]{:S(2)}) collective-permute-start(bf16[1,64,128]{2,1,0:T(8,128)(2,1)S(1)} %get-tuple-element.5), channel_id=1, source_target_pairs={{0,14},{2,12},{4,10},{6,8},{8,6},{10,4},{12,2},{14,0},{1,15},{3,13... | collective-permute-start | bytes 49160 | tf_op jit(solution)/shard_map/ppermute | solution.py:18
  88.8 5.6 %copy-start.6 = (f32[8]{0:T(128)S(1)}, f32[8]{0:T(128)}, u32[]{:S(2)}) copy-start(f32[8]{0:T(128)} %param.13) | copy-start | bytes 100
  94.4 18.5 %copy-start.3 = (f32[16,1,4,8,1]{0,3,2,1,4:T(8,128)}, f32[16,1,4,8,1]{0,3,2,1,4:T(8,128)S(1)}, u32[]{:S(2)}) copy-start(f32[16,1,4,8,1]{0,3,2,1,4:T(8,128)S(1)} %copy.18) | copy-start | bytes 6148
Sparse Core Ops, SparseCore 0:
  50.3 17.8 all-reduce.2
